TPU v7x, 512 devices: a whole 4x4x16 slice. The times are simulated.
512 devices in a mesh: wide: 32 (over z, core), narrow: 16 (over x, y).
Axes of the slice: x: 4, y: 4, z: 16, core: 2. Of those that a mesh axis runs over, the one named last changes fastest.
Arguments:
- activations: bfloat16 [512, 16384], P(None, 'wide'), may hold values from -6 to 6
- enc_weight: bfloat16 [16384, 16384], P('wide', 'narrow'), may hold values from -0.046875 to 0.046875
- enc_bias: float32 [16384], P('narrow'), may hold values from -4 to 4
- dec_weight: bfloat16 [16384, 16384], P('narrow', 'wide'), may hold values from -0.375 to 0.375
- dec_bias: float32 [16384], P('wide'), may hold values from -4 to 4
- active_ids: int32 [512, 64], replicated, may hold values from 0 to 16383, all different within a row
Outputs:
- dec_grad: bfloat16 [16384, 16384], P('narrow', 'wide')
- latent_grad: float32 [512, 16384], P('wide', 'narrow')
Inputs may be any that keep to these rules, and one draw needn't show every extreme that they name: `active_ids`: each row names 64 different latents; every latent is named by some row.
All inputs are finite; a program needn't handle non-finite values.
Results may differ from a plain program's by a relative error of at most 0.0058.
Values may be sent and summed in bfloat16 or wider, within the bound.
No kernel may reach another device: no remote copies, remote signals or barrier semaphores. Data moves between devices by JAX's collectives and lax.ppermute only.
A program may use at most 128 MiB of HBM per device.

v0:
```python
import jax
import jax.numpy as jnp
from jax import lax
from jax.sharding import Mesh
from jax.sharding import PartitionSpec as P

NARROW = ("narrow_0", "narrow_1")
WIDE = ("wide_0", "wide_1")


def filled_with(value, identity):
    return jnp.broadcast_to(jnp.asarray(identity, value.dtype), value.shape)


def carried_in(value, axes, combine, identity, reverse):
    before = start = filled_with(value, identity)
    total = value
    for axis in reversed(axes):
        length, position = (lax.axis_size(axis), lax.axis_index(axis))
        pieces = lax.all_gather(total, axis)
        inside, total = (start, start)
        for k in reversed(range(length)) if reverse else range(length):
            passed = k > position if reverse else k < position
            total = combine(total, pieces[k])
            inside = jnp.where(passed, total, inside)
        before = combine(inside, before)
    return before


def reduced_to_own(pieces, axes, turns):
    inside = pieces.shape[1:]
    pieces = pieces.reshape(*(lax.axis_size(a) for a in axes), *inside)
    pieces = jnp.moveaxis(pieces, turns, range(len(axes))).reshape(-1, *inside)
    for k in turns:
        pieces = lax.psum_scatter(pieces, axes[k], scatter_dimension=0, tiled=True)
    return pieces[0]


def in_blocks(value, dim, length):
    dims = value.shape
    pieces = value.reshape(*dims[:dim], length, dims[dim] // length, *dims[dim + 1 :])
    return jnp.moveaxis(pieces, dim, 0)


def summed_rows(value, axes, turns, dim):
    length = lax.axis_size(axes)
    return reduced_to_own(in_blocks(value, dim, length), axes, turns)


def add_fields(earlier, later):
    return jax.tree.map(jnp.add, earlier, later)


def local(activations, enc_weight, enc_bias, dec_weight, dec_bias, active_ids):
    token_count = activations.shape[0]
    latent_width = enc_weight.shape[1]
    groups = lax.axis_size(NARROW)
    group_index = lax.axis_index(NARROW)
    first_latent = group_index * latent_width
    inside = (active_ids >= first_latent) & (active_ids < first_latent + latent_width)
    local_ids = jnp.where(inside, active_ids - first_latent, latent_width)
    row_index = jnp.arange(token_count, dtype=jnp.int32)[:, None]
    active_mask = (
        jnp.zeros((token_count, latent_width), jnp.float32)
        .at[row_index, local_ids]
        .set(1.0, mode="drop")
    )
    share_rows = token_count // lax.axis_size(WIDE)
    offset = lax.axis_index(WIDE) * share_rows
    own_mask = lax.dynamic_slice_in_dim(active_mask, offset, share_rows, 0)
    partial_pre = jnp.dot(activations, enc_weight, preferred_element_type=jnp.float32)
    preact = lax.psum(partial_pre, WIDE) + enc_bias
    latents = (active_mask * preact).astype(jnp.bfloat16)
    recon_part = jnp.dot(latents, dec_weight, preferred_element_type=jnp.float32)
    target = activations.astype(jnp.float32)
    nothing = jnp.zeros_like(recon_part)
    before = carried_in(recon_part, NARROW, add_fields, nothing, False)
    errors_here = dec_bias + before + recon_part - target
    later_sum = carried_in(errors_here, NARROW, add_fields, nothing, True)
    suffix = later_sum + errors_here
    errors = (suffix / groups).astype(jnp.bfloat16)
    dec_grad = lax.dot_general(
        latents, errors, (((0,), (0,)), ((), ())), preferred_element_type=jnp.float32
    ).astype(jnp.bfloat16)
    latent_rows = summed_rows(
        lax.dot_general(
            errors, dec_weight, (((1,), (1,)), ((), ())), preferred_element_type=jnp.float32
        ),
        WIDE,
        (1, 0),
        0,
    )
    latent_out = own_mask * latent_rows
    return (dec_grad, latent_out)


def solution(mesh):
    split = Mesh(mesh.devices.reshape(16, 2, 4, 4), ("wide_0", "wide_1", "narrow_0", "narrow_1"))
    return jax.shard_map(
        local,
        mesh=split,
        in_specs=(P(None, WIDE), P(WIDE, NARROW), P(NARROW), P(NARROW, WIDE), P(WIDE), P()),
        out_specs=(P(NARROW, WIDE), P(WIDE, NARROW)),
        check_vma=False,
    )
```

profile of v0, /device:TPU:2, one launch (start us, length us, event | category | flops | bytes accessed | tf_op | source)
XLA Modules:
  0.0 583.1 jit_solution(8263159260602203690)
XLA Ops:
  7.2 0.0 copy-start
  7.2 0.0 copy-start.7
  7.2 0.0 all-reduce.2.cloned.1.call-start
  7.2 3.5 fusion.17
  10.8 0.0 copy-start.11
  10.8 0.0 copy-start.10
  10.8 0.0 all-reduce.2.cloned.1.call-update
  10.8 0.0 all-gather.11.cloned.1.call-start
  10.8 0.0 copy-done.7
  10.9 0.5 copy-done.11
  11.4 0.1 multiply_reduce_fusion
  11.5 0.0 copy-done.10
  11.5 0.1 and_reduce_fusion
  11.7 0.1 copy.10
  11.8 0.1 reshape.66
  11.9 121.5 %scatter_custom_fusion = f32[524288]{0:T(1024)} fusion(s32[32768]{0:T(1024)S(1)} %reshape.66, f32[32768]{0:T(1024)S(1)} %broadcast.52, f32[]{:T(128)} %constant.17.clone.1), kind=kCustom, calls=%fused_computation.31 | custom fusion | bytes 2097156
  133.4 0.0 copy-start.8
  133.4 1.7 reshape.63
  135.1 0.0 copy-start.2
  135.1 94.1 %all-reduce.2.cloned.1.call-done = f32[512,1024]{1,0:T(8,128)} async-done(((f32[512,1024]{1,0:T(8,128)}), f32[512,1024]{1,0:T(8,128)}) %all-reduce.2.cloned.1.call-update) | async-done | bytes 2097168 | tf_op jit(solution)/shard_map/psum | solution.py:72
  229.2 0.0 copy-done.8
  229.2 2.1 multiply_convert_fusion
  231.3 0.0 copy-done.2
  231.3 0.0 copy-start.5
  231.3 1.0 copy-done.5
  232.3 0.0 copy-done
  232.3 1.7 fusion.18
  234.0 0.0 all-gather.11.cloned.1.call-update
  234.0 0.0 copy-start.3
  234.0 0.0 copy-start.4
  234.0 0.0 copy-start.9
  234.0 0.0 all-gather.7.cloned.1.call-start
  234.1 56.1 %all-gather.11.cloned.1.call-done = f32[2048,512]{1,0:T(8,128)} async-done(((f32[512,512]{1,0:T(8,128)}), f32[2048,512]{1,0:T(8,128)}) %all-gather.11.cloned.1.call-update) | async-done | bytes 4194320 | tf_op jit(solution)/shard_map/all_gather | solution.py:20
  290.1 3.7 fusion.13
  293.8 0.0 all-gather.7.cloned.1.call-update
  293.8 0.0 all-gather.13.cloned.1.call-start
  293.9 55.8 %all-gather.7.cloned.1.call-done = f32[4,512,512]{2,1,0:T(8,128)} async-done(((f32[1,512,512]{2,1,0:T(8,128)}), f32[4,512,512]{2,1,0:T(8,128)}) %all-gather.7.cloned.1.call-update) | async-done | bytes 4194320 | tf_op jit(solution)/shard_map/all_gather | solution.py:20
  349.7 0.0 copy-done.3
  349.7 0.0 copy-done.4
  349.7 0.0 copy-done.9
  349.7 5.6 fusion.12
  355.3 0.0 all-gather.13.cloned.1.call-update
  355.3 0.0 copy-start.1
  355.3 0.0 all-gather.9.cloned.1.call-start
  355.4 57.1 %all-gather.13.cloned.1.call-done = f32[2048,512]{1,0:T(8,128)} async-done(((f32[512,512]{1,0:T(8,128)}), f32[2048,512]{1,0:T(8,128)}) %all-gather.13.cloned.1.call-update) | async-done | bytes 4194320 | tf_op jit(solution)/shard_map/all_gather | solution.py:20
  412.5 3.7 fusion.6
  416.1 0.0 all-gather.9.cloned.1.call-update
  416.2 0.0 reduce-scatter.3.cloned.1.call-start
  416.2 55.8 %all-gather.9.cloned.1.call-done = f32[4,512,512]{2,1,0:T(8,128)} async-done(((f32[1,512,512]{2,1,0:T(8,128)}), f32[4,512,512]{2,1,0:T(8,128)}) %all-gather.9.cloned.1.call-update) | async-done | bytes 4194320 | tf_op jit(solution)/shard_map/all_gather | solution.py:20
  472.0 0.0 copy-done.1
  472.0 4.6 fusion.5
  476.6 0.7 fusion.19
  477.4 1.5 copy.11
  478.8 0.0 copy-start.6
  478.8 0.0 reduce-scatter.3.cloned.1.call-update
  478.9 0.0 reduce-scatter.5.cloned.1.call-start
  478.9 21.2 %reduce-scatter.3.cloned.1.call-done = f32[16,16,1024]{2,1,0:T(8,128)} async-done(((f32[32,16,1024]{2,1,0:T(8,128)}), f32[16,16,1024]{2,1,0:T(8,128)}) %reduce-scatter.3.cloned.1.call-update) | async-done | bytes 1048592 | tf_op jit(solution)/shard_map/reduce_scatter | solution.py:35
  500.1 0.0 reduce-scatter.5.cloned.1.call-update
  500.2 0.0 copy-done.6
  500.2 1.7 convolution_convert_fusion
  501.9 72.8 %reduce-scatter.5.cloned.1.call-done = f32[1,16,1024]{2,1,0:T(8,128)} async-done(((f32[16,16,1024]{2,1,0:T(8,128)}), f32[1,16,1024]{2,1,0:T(8,128)}) %reduce-scatter.5.cloned.1.call-update) | async-done | bytes 65552 | tf_op jit(solution)/shard_map/reduce_scatter | solution.py:35
  574.7 1.5 bitcast_multiply_fusion
  (4 shorter events, 0.1 us)
Async XLA Ops:
  7.2 225.1 %copy-start = (bf16[1024,512]{1,0:T(8,128)(2,1)S(1)}, bf16[1024,512]{1,0:T(8,128)(2,1)}, u32[]{:S(2)}) copy-start(bf16[1024,512]{1,0:T(8,128)(2,1)} %param.9) | copy-start | bytes 3145732
  7.2 3.7 copy-start.7
  7.2 222.0 %all-reduce.2.cloned.1.call-start = ((), (), s32[]{:S(2)}) async-start(), calls=%async_computation.2 | async-start | bytes 4194304 | tf_op jit(solution)/shard_map/psum | solution.py:72
  10.8 0.7 copy-start.11
  10.8 0.7 copy-start.10
  10.8 279.3 %all-gather.11.cloned.1.call-start = ((), (), s32[]{:S(2)}) async-start(), calls=%async_computation.7 | async-start | bytes 5242880 | tf_op jit(solution)/shard_map/all_gather | solution.py:20
  133.4 95.8 %copy-start.8 = (f32[1024]{0:T(1024)S(1)}, f32[1024]{0:T(1024)}, u32[]{:S(2)}) copy-start(f32[1024]{0:T(1024)} %param.8) | copy-start | bytes 12292
  135.1 96.2 %copy-start.2 = (f32[512,1024]{1,0:T(8,128)}, f32[512,1024]{1,0:T(8,128)S(1)}, u32[]{:S(2)}) copy-start(f32[512,1024]{1,0:T(8,128)S(1)} %reshape.63) | copy-start | bytes 6291460
  231.3 1.0 copy-start.5
  234.0 115.7 %copy-start.3 = (f32[512,512]{1,0:T(8,128)S(1)}, f32[512,512]{1,0:T(8,128)}, u32[]{:S(2)}) copy-start(f32[512,512]{1,0:T(8,128)} %fusion.18) | copy-start | bytes 3145732
  234.0 115.7 %copy-start.4 = (bf16[512,512]{1,0:T(8,128)(2,1)S(1)}, bf16[512,512]{1,0:T(8,128)(2,1)}, u32[]{:S(2)}) copy-start(bf16[512,512]{1,0:T(8,128)(2,1)} %param.6) | copy-start | bytes 1572868
  234.0 115.7 %copy-start.9 = (f32[512]{0:T(512)S(1)}, f32[512]{0:T(512)}, u32[]{:S(2)}) copy-start(f32[512]{0:T(512)} %param.10) | copy-start | bytes 6148
  234.0 115.6 %all-gather.7.cloned.1.call-start = ((), (), s32[]{:S(2)}) async-start(), calls=%async_computation.3 | async-start | bytes 5242880 | tf_op jit(solution)/shard_map/all_gather | solution.py:20
  293.8 118.7 %all-gather.13.cloned.1.call-start = ((), (), s32[]{:S(2)}) async-start(), calls=%async_computation.8 | async-start | bytes 5242880 | tf_op jit(solution)/shard_map/all_gather | solution.py:20
  355.3 116.7 %copy-start.1 = (f32[512,512]{1,0:T(8,128)S(1)}, f32[512,512]{1,0:T(8,128)}, u32[]{:S(2)}) copy-start(f32[512,512]{1,0:T(8,128)} %fusion.12) | copy-start | bytes 3145732
  355.3 116.7 %all-gather.9.cloned.1.call-start = ((), (), s32[]{:S(2)}) async-start(), calls=%async_computation.4 | async-start | bytes 5242880 | tf_op jit(solution)/shard_map/all_gather | solution.py:20
  416.2 84.0 %reduce-scatter.3.cloned.1.call-start = ((), (), s32[]{:S(2)}) async-start(), calls=%async_computation.5 | async-start | bytes 3145728 | tf_op jit(solution)/shard_map/reduce_scatter | solution.py:35
  478.8 21.3 %copy-start.6 = (bf16[512,1024]{1,0:T(8,128)(2,1)S(1)}, bf16[512,1024]{1,0:T(8,128)(2,1)}, u32[]{:S(2)}) copy-start(bf16[512,1024]{1,0:T(8,128)(2,1)} %copy-done.5) | copy-start | bytes 3145732
  478.9 95.9 %reduce-scatter.5.cloned.1.call-start = ((), (), s32[]{:S(2)}) async-start(), calls=%async_computation.6 | async-start | bytes 1114112 | tf_op jit(solution)/shard_map/reduce_scatter | solution.py:35
Sparse Core Ops, SparseCore 0:
  10.9 218.2 all-reduce.1
  234.1 55.9 all-gather.10
  293.9 55.6 all-gather.6
  355.4 57.0 all-gather.12
  416.3 55.6 all-gather.8
  479.0 21.1 reduce-scatter.2
  502.9 71.7 reduce-scatter.4
where the time goes:
time: 583 us
  waiting for transfers between devices  413 us (71%)
  local copies, waits for them, and re-layouts  126 us (22%)
  other arithmetic  21.4 us (4%)
  between operations  14.3 us (2%)
  matrix products  7.66 us (1%)
    all_gather x4, waiting for transfers between devices, carried_in(): pieces = lax.all_gather(total, axis)  225 us
    unnamed x28, local copies, waits for them, and re-layouts  123 us
    reduce_scatter x2, waiting for transfers between devices, reduced_to_own(): pieces = lax.psum_scatter(pieces, axes[k], scatter_dimension=0, tiled=True)  94.1 us
    psum x1, waiting for transfers between devices, local(): preact = lax.psum(partial_pre, WIDE) + enc_bias  94.1 us
  transfers between devices with their start and end apart: 7, of which 7 were waited for; matrix products, arithmetic and copies ran while one was open for 22% of the time, Pallas kernels for 0%

commit v1 on v0

--- a/solution.py
+++ b/solution.py
@@ -69,7 +69,7 @@
     offset = lax.axis_index(WIDE) * share_rows
     own_mask = lax.dynamic_slice_in_dim(active_mask, offset, share_rows, 0)
     partial_pre = jnp.dot(activations, enc_weight, preferred_element_type=jnp.float32)
-    preact = lax.psum(partial_pre, WIDE) + enc_bias
+    preact = lax.psum(lax.psum(partial_pre, "wide_0"), "wide_1") + enc_bias
     latents = (active_mask * preact).astype(jnp.bfloat16)
     recon_part = jnp.dot(latents, dec_weight, preferred_element_type=jnp.float32)
     target = activations.astype(jnp.float32)

time: 583 us -> 634 us (1.087)
  waiting for transfers between devices: 413 us -> 464 us
    psum x1 -> x2, waiting for transfers between devices: 94.1 us -> 149 us  [local(): preact = lax.psum(lax.psum(partial_pre, 'wide_0'), 'wide_1') + enc_bias]
  transfers between devices with their start and end apart: 7 -> 8, of which waited for: 7 -> 7; matrix products, arithmetic and copies ran while one was open for 22% -> 20% of each run, Pallas kernels for 0% -> 0%
where the time goes in v1:
time: 634 us
  waiting for transfers between devices  464 us (73%)
  local copies, waits for them, and re-layouts  126 us (20%)
  other arithmetic  22.1 us (3%)
  between operations  14.4 us (2%)
  matrix products  7.64 us (1%)
    all_gather x4, waiting for transfers between devices, carried_in(): pieces = lax.all_gather(total, axis)  221 us
    psum x2, waiting for transfers between devices, local(): preact = lax.psum(lax.psum(partial_pre, 'wide_0'), 'wide_1') + enc_bias  149 us
    unnamed x28, local copies, waits for them, and re-layouts  123 us
    reduce_scatter x2, waiting for transfers between devices, reduced_to_own(): pieces = lax.psum_scatter(pieces, axes[k], scatter_dimension=0, tiled=True)  94.1 us
  transfers between devices with their start and end apart: 8, of which 7 were waited for; matrix products, arithmetic and copies ran while one was open for 20% of the time, Pallas kernels for 0%

profile of v1, /device:TPU:2, one launch (start us, length us, event | category | flops | bytes accessed | tf_op | source)
XLA Modules:
  0.0 634.0 jit_solution(17261515234664240268)
XLA Ops:
  7.2 0.0 copy-start
  7.2 0.0 all-reduce.3.cloned.1.call-start
  7.2 3.5 fusion.17
  10.7 0.0 copy-start.7
  10.7 0.0 copy-start.11
  10.7 0.0 copy-start.10
  10.7 0.0 all-reduce.3.cloned.1.call-update
  10.8 0.0 all-reduce.5.cloned.1.call-start
  10.8 148.6 %all-reduce.3.cloned.1.call-done = f32[512,1024]{1,0:T(8,128)} async-done(((f32[512,1024]{1,0:T(8,128)}), f32[512,1024]{1,0:T(8,128)}) %all-reduce.3.cloned.1.call-update) | async-done | bytes 2097168 | tf_op jit(solution)/shard_map/psum | solution.py:72
  159.4 0.0 all-reduce.5.cloned.1.call-update
  159.4 0.0 all-gather.11.cloned.1.call-start
  159.5 0.0 copy-done.7
  159.5 0.0 copy-done.11
  159.6 0.1 multiply_reduce_fusion
  159.6 0.0 copy-done.10
  159.7 0.1 and_reduce_fusion
  159.8 0.1 copy.10
  159.9 0.1 reshape.66
  160.1 121.5 %scatter_custom_fusion = f32[524288]{0:T(1024)} fusion(s32[32768]{0:T(1024)S(1)} %reshape.66, f32[32768]{0:T(1024)S(1)} %broadcast.52, f32[]{:T(128)} %constant.17.clone.1), kind=kCustom, calls=%fused_computation.31 | custom fusion | bytes 2097156
  281.5 0.0 copy-start.8
  281.5 1.7 reshape.63
  283.3 0.0 copy-start.2
  283.3 0.0 all-reduce.5.cloned.1.call-done
  283.3 0.0 copy-done.8
  283.3 2.8 multiply_convert_fusion
  286.1 0.0 copy-done.2
  286.2 0.0 copy-start.5
  286.2 1.0 copy-done.5
  287.1 0.0 copy-done
  287.1 1.7 fusion.18
  288.8 0.0 all-gather.11.cloned.1.call-update
  288.8 0.0 copy-start.3
  288.8 0.0 copy-start.4
  288.9 0.0 copy-start.9
  288.9 0.0 all-gather.7.cloned.1.call-start
  288.9 52.1 %all-gather.11.cloned.1.call-done = f32[2048,512]{1,0:T(8,128)} async-done(((f32[512,512]{1,0:T(8,128)}), f32[2048,512]{1,0:T(8,128)}) %all-gather.11.cloned.1.call-update) | async-done | bytes 4194320 | tf_op jit(solution)/shard_map/all_gather | solution.py:20
  341.1 3.7 fusion.13
  344.7 0.0 all-gather.7.cloned.1.call-update
  344.8 0.0 all-gather.13.cloned.1.call-start
  344.8 55.8 %all-gather.7.cloned.1.call-done = f32[4,512,512]{2,1,0:T(8,128)} async-done(((f32[1,512,512]{2,1,0:T(8,128)}), f32[4,512,512]{2,1,0:T(8,128)}) %all-gather.7.cloned.1.call-update) | async-done | bytes 4194320 | tf_op jit(solution)/shard_map/all_gather | solution.py:20
  400.6 0.0 copy-done.3
  400.6 0.0 copy-done.4
  400.6 0.0 copy-done.9
  400.6 5.6 fusion.12
  406.2 0.0 all-gather.13.cloned.1.call-update
  406.2 0.0 copy-start.1
  406.3 0.0 all-gather.9.cloned.1.call-start
  406.3 57.1 %all-gather.13.cloned.1.call-done = f32[2048,512]{1,0:T(8,128)} async-done(((f32[512,512]{1,0:T(8,128)}), f32[2048,512]{1,0:T(8,128)}) %all-gather.13.cloned.1.call-update) | async-done | bytes 4194320 | tf_op jit(solution)/shard_map/all_gather | solution.py:20
  463.4 3.7 fusion.6
  467.1 0.0 all-gather.9.cloned.1.call-update
  467.1 0.0 reduce-scatter.3.cloned.1.call-start
  467.2 55.8 %all-gather.9.cloned.1.call-done = f32[4,512,512]{2,1,0:T(8,128)} async-done(((f32[1,512,512]{2,1,0:T(8,128)}), f32[4,512,512]{2,1,0:T(8,128)}) %all-gather.9.cloned.1.call-update) | async-done | bytes 4194320 | tf_op jit(solution)/shard_map/all_gather | solution.py:20
  522.9 0.0 copy-done.1
  523.0 4.6 fusion.5
  527.6 0.7 fusion.19
  528.3 1.5 copy.11
  529.8 0.0 reduce-scatter.3.cloned.1.call-update
  529.8 0.0 reduce-scatter.5.cloned.1.call-start
  529.8 21.2 %reduce-scatter.3.cloned.1.call-done = f32[16,16,1024]{2,1,0:T(8,128)} async-done(((f32[32,16,1024]{2,1,0:T(8,128)}), f32[16,16,1024]{2,1,0:T(8,128)}) %reduce-scatter.3.cloned.1.call-update) | async-done | bytes 1048592 | tf_op jit(solution)/shard_map/reduce_scatter | solution.py:35
  551.1 0.0 reduce-scatter.5.cloned.1.call-update
  551.1 0.0 copy-done.6
  551.1 1.7 convolution_convert_fusion
  552.8 72.8 %reduce-scatter.5.cloned.1.call-done = f32[1,16,1024]{2,1,0:T(8,128)} async-done(((f32[16,16,1024]{2,1,0:T(8,128)}), f32[1,16,1024]{2,1,0:T(8,128)}) %reduce-scatter.5.cloned.1.call-update) | async-done | bytes 65552 | tf_op jit(solution)/shard_map/reduce_scatter | solution.py:35
  625.7 1.5 bitcast_multiply_fusion
  (5 shorter events, 0.1 us)
Async XLA Ops:
  7.2 280.0 %copy-start = (bf16[1024,512]{1,0:T(8,128)(2,1)S(1)}, bf16[1024,512]{1,0:T(8,128)(2,1)}, u32[]{:S(2)}) copy-start(bf16[1024,512]{1,0:T(8,128)(2,1)} %param.9) | copy-start | bytes 3145732
  7.2 152.2 %all-reduce.3.cloned.1.call-start = ((), (), s32[]{:S(2)}) async-start(), calls=%async_computation.2 | async-start | bytes 4194304 | tf_op jit(solution)/shard_map/psum | solution.py:72
  10.7 148.7 %copy-start.7 = (s32[512,64]{0,1:T(8,128)S(1)}, s32[512,64]{0,1:T(8,128)}, u32[]{:S(2)}) copy-start(s32[512,64]{0,1:T(8,128)} %param.11) | copy-start | bytes 393220
  10.7 148.8 %copy-start.11 = (s32[2]{0:T(128)S(1)}, s32[2]{0:T(128)}, u32[]{:S(2)}) copy-start(s32[2]{0:T(128)} %constant.47) | copy-start | bytes 28
  10.7 148.9 %copy-start.10 = (s32[2]{0:T(128)S(1)}, s32[2]{0:T(128)}, u32[]{:S(2)}) copy-start(s32[2]{0:T(128)} %constant.50) | copy-start | bytes 28
  10.8 272.6 %all-reduce.5.cloned.1.call-start = ((), (), s32[]{:S(2)}) async-start(), calls=%async_computation.3 | async-start | bytes 4194304 | tf_op jit(solution)/shard_map/psum | solution.py:72
  159.4 181.7 %all-gather.11.cloned.1.call-start = ((), (), s32[]{:S(2)}) async-start(), calls=%async_computation.8 | async-start | bytes 5242880 | tf_op jit(solution)/shard_map/all_gather | solution.py:20
  281.5 1.8 copy-start.8
  283.3 2.9 copy-start.2
  286.2 1.0 copy-start.5
  288.8 111.8 %copy-start.3 = (f32[512,512]{1,0:T(8,128)S(1)}, f32[512,512]{1,0:T(8,128)}, u32[]{:S(2)}) copy-start(f32[512,512]{1,0:T(8,128)} %fusion.18) | copy-start | bytes 3145732
  288.8 111.8 %copy-start.4 = (bf16[512,512]{1,0:T(8,128)(2,1)S(1)}, bf16[512,512]{1,0:T(8,128)(2,1)}, u32[]{:S(2)}) copy-start(bf16[512,512]{1,0:T(8,128)(2,1)} %param.6) | copy-start | bytes 1572868
  288.9 111.8 %copy-start.9 = (f32[512]{0:T(512)S(1)}, f32[512]{0:T(512)}, u32[]{:S(2)}) copy-start(f32[512]{0:T(512)} %param.10) | copy-start | bytes 6148
  288.9 111.7 %all-gather.7.cloned.1.call-start = ((), (), s32[]{:S(2)}) async-start(), calls=%async_computation.4 | async-start | bytes 5242880 | tf_op jit(solution)/shard_map/all_gather | solution.py:20
  344.8 118.7 %all-gather.13.cloned.1.call-start = ((), (), s32[]{:S(2)}) async-start(), calls=%async_computation.9 | async-start | bytes 5242880 | tf_op jit(solution)/shard_map/all_gather | solution.py:20
  406.2 116.7 %copy-start.1 = (f32[512,512]{1,0:T(8,128)S(1)}, f32[512,512]{1,0:T(8,128)}, u32[]{:S(2)}) copy-start(f32[512,512]{1,0:T(8,128)} %fusion.12) | copy-start | bytes 3145732
  406.3 116.7 %all-gather.9.cloned.1.call-start = ((), (), s32[]{:S(2)}) async-start(), calls=%async_computation.5 | async-start | bytes 5242880 | tf_op jit(solution)/shard_map/all_gather | solution.py:20
  467.1 84.0 %reduce-scatter.3.cloned.1.call-start = ((), (), s32[]{:S(2)}) async-start(), calls=%async_computation.6 | async-start | bytes 3145728 | tf_op jit(solution)/shard_map/reduce_scatter | solution.py:35
  529.8 21.3 %copy-start.6 = (bf16[512,1024]{1,0:T(8,128)(2,1)S(1)}, bf16[512,1024]{1,0:T(8,128)(2,1)}, u32[]{:S(2)}) copy-start(bf16[512,1024]{1,0:T(8,128)(2,1)} %copy-done.5) | copy-start | bytes 3145732
  529.8 95.9 %reduce-scatter.5.cloned.1.call-start = ((), (), s32[]{:S(2)}) async-start(), calls=%async_computation.7 | async-start | bytes 1114112 | tf_op jit(solution)/shard_map/reduce_scatter | solution.py:35
Sparse Core Ops, SparseCore 0:
  10.9 148.4 all-reduce.2
  162.3 38.3 all-reduce.4
  289.0 52.0 all-gather.10
  344.9 55.6 all-gather.6
  406.4 57.0 all-gather.12
  467.2 55.6 all-gather.8
  529.9 21.1 reduce-scatter.2
  553.9 71.7 reduce-scatter.4
